TPU v7x, 256 devices: a whole 4x4x8 slice. The times are simulated.
256 devices in a mesh: section: 2 (over core), expert: 128 (over y, x, z).
Axes of the slice: x: 4, y: 4, z: 8, core: 2. Of those that a mesh axis runs over, the one named last changes fastest.
Arguments:
- source_tokens: bfloat16 [32768, 2048], P(('section', 'expert')), may hold values from -6 to 6
- routes: int32 [32768, 2], P(('section', 'expert')), may hold values from 0 to 63, all different within a row; in each aligned block of 128 rows (0 to 127, 128 to 255, ...) at most 5 rows name the same one
- gates: float32 [32768, 2], P(('section', 'expert')), may hold values from 0.1 to 1
- source_sentence: int32 [256, 128], P(('section', 'expert')), may hold values from 0 to 3, never falling along the last dimension, each value on 1 to 64 neighbouring positions
- expert_in: bfloat16 [128, 2048, 2048], P('expert', None, 'section'), may hold values from -0.125 to 0.125
- expert_out: bfloat16 [128, 2048, 2048], P('expert', 'section'), may hold values from -0.09375 to 0.09375
- final_gain: float32 [2048], replicated, may hold values from 0.1 to 1.9
- target_tokens: bfloat16 [65536, 2048], P(('section', 'expert')), may hold values from -256 to 256
- target_sentence: int32 [256, 256], P(('section', 'expert')), may hold values from 0 to 3, never falling along the last dimension, each value on 1 to 128 neighbouring positions
- query_weight: bfloat16 [2048, 1024], P(('section', 'expert')), may hold values from -0.125 to 0.125
- key_weight: bfloat16 [2048, 1024], P(('section', 'expert')), may hold values from -0.125 to 0.125
- value_weight: bfloat16 [2048, 1024], P(('section', 'expert')), may hold values from -0.125 to 0.125
Outputs:
- memory: bfloat16 [32768, 2048], P(('section', 'expert'))
- context: bfloat16 [65536, 1024], P(('section', 'expert'))
Inputs may be any that keep to these rules, and one draw needn't show every extreme that they name: `routes`: each row names two different experts; among the 128 rows of one device no expert is named more than 5 times, a bound that some block reaches. `source_sentence`: within a block the numbers never fall and all 4 sentences appear. `target_sentence`: within a block the numbers never fall and all 4 sentences appear.
All inputs are finite; a program needn't handle non-finite values.
Results may differ from a plain program's by a relative error of at most 0.035.
Values may be sent and summed in bfloat16 or wider, within the bound.
A program may use at most 128 MiB of HBM per device.

v0:
```python
import jax
import jax.numpy as jnp
from jax import lax
from jax.sharding import PartitionSpec as P

HEADS = 8
HDIM = 128


def swapped(block, axis, stride):
    count = lax.axis_size(axis)
    route = []
    for low in range(count):
        high = low | 1 << stride
        if high != low and high < count:
            route += [(low, high), (high, low)]
    return lax.ppermute(block, axis, route)


def layer_norm(values):
    mean = jnp.mean(values, axis=-1, keepdims=True)
    centred = values - mean
    spread = jnp.mean(centred * centred, axis=-1, keepdims=True)
    return centred * lax.rsqrt(spread + 1e-05)


def expert_pass(rows, first_weight, second_weight):
    hidden = jnp.maximum(
        jnp.dot(rows, first_weight, preferred_element_type=jnp.float32), 0.0
    ).astype(jnp.bfloat16)
    return jnp.dot(hidden, second_weight, preferred_element_type=jnp.float32)


def body(
    source_tokens,
    routes,
    gates,
    source_sentence,
    expert_in,
    expert_out,
    final_gain,
    target_tokens,
    target_sentence,
    query_weight,
    key_weight,
    value_weight,
):
    groups = lax.axis_size("expert")
    experts = groups // 2
    rows_here = source_tokens.shape[0]
    width = source_tokens.shape[1]
    capacity = 5 * rows_here // (2 * experts)
    normed = layer_norm(source_tokens.astype(jnp.float32)).astype(jnp.bfloat16)
    flat = routes.reshape(-1)
    picks = (flat[:, None] == jnp.arange(experts, dtype=jnp.int32)[None, :]).astype(jnp.int32)
    places = jnp.sum((jnp.cumsum(picks, axis=0) - 1) * picks, axis=1)
    slot_of = flat * capacity + places
    dispatch = jnp.arange(experts * capacity, dtype=jnp.int32)[:, None] == slot_of[None, :]
    copies = jnp.repeat(normed, 2, axis=0)
    packed = jnp.dot(
        dispatch.astype(jnp.bfloat16), copies, preferred_element_type=jnp.float32
    ).astype(jnp.bfloat16)
    doubled = jnp.repeat(packed.reshape(experts, capacity, width), 2, axis=0).reshape(
        groups * capacity, width
    )
    arriving = lax.all_to_all(doubled, "expert", split_axis=0, concat_axis=0, tiled=True)
    whole_in, whole_out = (
        lax.all_gather(expert_in, "section", axis=2, tiled=True),
        lax.all_gather(expert_out, "section", axis=1, tiled=True),
    )
    half_sum = expert_pass(arriving, whole_in[0], whole_out[0])
    returned = lax.all_to_all(half_sum, "expert", split_axis=0, concat_axis=0, tiled=True)
    shaped = returned.reshape(experts, 2, capacity, width)
    expert_rows = (shaped[:, 0] + shaped[:, 1]).reshape(experts * capacity, width)
    per_route = jnp.dot(
        dispatch.astype(jnp.float32).T, expert_rows, precision=lax.Precision.HIGHEST
    )
    mixture = jnp.sum(per_route.reshape(rows_here, 2, width) * gates[:, :, None], axis=1)
    updated = source_tokens.astype(jnp.float32) + mixture
    memory = (layer_norm(updated) * final_gain).astype(jnp.bfloat16)
    partner_memory, partner_sentence = swapped((memory, source_sentence), "section", 0)
    head_width = query_weight.shape[1]
    target_rows = target_tokens.shape[0]
    key_rows = partner_memory.shape[0]
    queries = jnp.dot(
        target_tokens,
        lax.all_gather(query_weight, ("section", "expert"), axis=0, tiled=True),
        preferred_element_type=jnp.float32,
    )
    keys = jnp.dot(
        partner_memory,
        lax.all_gather(key_weight, ("section", "expert"), axis=0, tiled=True),
        preferred_element_type=jnp.float32,
    )
    values = jnp.dot(
        partner_memory,
        lax.all_gather(value_weight, ("section", "expert"), axis=0, tiled=True),
        preferred_element_type=jnp.float32,
    )
    queries = queries.astype(jnp.bfloat16).reshape(target_rows, HEADS, HDIM)
    keys = keys.astype(jnp.bfloat16).reshape(key_rows, HEADS, HDIM)
    values = values.astype(jnp.bfloat16).reshape(key_rows, HEADS, HDIM)
    scores = jnp.einsum("qhd,khd->hqk", queries, keys, preferred_element_type=jnp.float32) * (
        1.0 / HDIM**0.5
    )
    same = (target_sentence[0][:, None] == partner_sentence[0][None, :])[None, :, :]
    scores = jnp.where(same, scores, -jnp.inf)
    peak = jnp.max(scores, axis=-1, keepdims=True)
    raised = jnp.exp(scores - peak)
    probs = (raised / jnp.sum(raised, axis=-1, keepdims=True)).astype(jnp.bfloat16)
    mixed = jnp.einsum("hqk,khd->qhd", probs, values, preferred_element_type=jnp.float32)
    return (memory, mixed.reshape(target_rows, head_width).astype(jnp.bfloat16))


def solution(mesh):
    placed = (
        P(("section", "expert"), None),
        P(("section", "expert"), None),
        P(("section", "expert"), None),
        P(("section", "expert"), None),
        P("expert", None, "section"),
        P("expert", "section", None),
        P(),
        P(("section", "expert"), None),
        P(("section", "expert"), None),
        P(("section", "expert"), None),
        P(("section", "expert"), None),
        P(("section", "expert"), None),
    )
    return jax.shard_map(
        body,
        mesh=mesh,
        in_specs=placed,
        out_specs=(P(("section", "expert"), None), P(("section", "expert"), None)),
        check_vma=False,
    )
```

profile of v0, /device:TPU:1, one launch (start us, length us, event | category | flops | bytes accessed | tf_op | source)
XLA Modules:
  0.0 462.7 jit_solution(13492900357546544288)
XLA Ops:
  7.2 0.0 copy-start
  7.2 0.0 copy-start.4
  7.2 0.0 copy-start.1
  7.2 0.0 all-gather.6.cloned.1.call-start
  7.2 0.7 all-gather.6.cloned.1.call-update
  7.9 0.0 all-gather.8.cloned.1.call-start
  8.0 0.7 all-gather.8.cloned.1.call-update
  8.7 0.0 all-gather.12.cloned.1.call-start
  8.7 0.7 all-gather.12.cloned.1.call-update
  9.4 0.0 copy-done.4
  9.4 0.1 copy.33
  9.5 0.1 eq.74
  9.7 0.1 reshape.149
  9.8 0.6 reduce-window.6
  10.5 0.2 slice_reduce_fusion
  10.7 0.2 convert_reduce_fusion
  10.9 0.3 fusion.16
  11.2 0.3 fusion.17
  11.5 0.6 broadcast_in_dim.12
  12.1 1.2 reshape.151
  13.4 0.1 fusion.34
  13.5 1.7 convolution_convert_fusion
  15.2 1.6 reshape.152
  16.8 4.1 broadcast_in_dim.13
  20.9 16.9 %all-to-all-start = ((bf16[128,5,2048]{2,1,0:T(8,128)(2,1)}), bf16[128,5,2048]{2,1,0:T(8,128)(2,1)}, u32[]{:S(2)}, u32[]{:S(2)}) async-start(bf16[128,5,2048]{2,1,0:T(8,128)(2,1)} %bitcast.74), calls=%async_computation | async-start | bytes 8388608 | tf_op jit(solution)/shard_map/all_to_all | solution.py:66
  37.8 0.2 all-gather.14.cloned.1.call-start
  38.0 0.3 all-gather.14.cloned.1.call-update
  38.4 96.3 %all-to-all-done = bf16[128,5,2048]{2,1,0:T(8,128)(2,1)} async-done(((bf16[128,5,2048]{2,1,0:T(8,128)(2,1)}), bf16[128,5,2048]{2,1,0:T(8,128)(2,1)}, u32[]{:S(2)}, u32[]{:S(2)}) %all-to-all-start) | async-done | bytes 2621472 | tf_op jit(solution)/shard_map/all_to_all | solution.py:66
  134.7 5.6 %all_to_all.14 = bf16[640,2048]{1,0:T(8,128)(2,1)} reshape(bf16[128,5,2048]{2,1,0:T(8,128)(2,1)} %all-to-all-done) | data formatting | bytes 5242880 | tf_op jit(solution)/shard_map/all_to_all | solution.py:66
  140.3 10.7 %maximum_convert_fusion = bf16[640,2048]{1,0:T(8,128)(2,1)} fusion(bf16[640,2048]{1,0:T(8,128)(2,1)} %all_to_all.14, bf16[1,2048,2048]{2,1,0:T(8,128)(2,1)} %all-gather.6.cloned.1.call-done), kind=kOutput, calls=%fused_computation.5 | convolution fusion | flops 5371330560 | bytes 13631488 | tf_op jit(solution)/shard_map/dot_general | solution.py:29
  151.0 5.5 %dot_general.31 = bf16[128,5,2048]{2,1,0:T(8,128)(2,1)} reshape(bf16[640,2048]{1,0:T(8,128)(2,1)} %maximum_convert_fusion) | data formatting | bytes 5242880 | tf_op jit(solution)/shard_map/dot_general | solution.py:31
  156.4 12.7 %fusion.1 = f32[128,5,2048]{2,0,1:T(8,128)S(1)} fusion(bf16[1,2048,2048]{2,1,0:T(8,128)(2,1)} %all-gather.8.cloned.1.call-done, bf16[128,5,2048]{2,1,0:T(8,128)(2,1)} %dot_general.31), kind=kOutput, calls=%fused_computation.1 | convolution fusion | flops 5368709120 | bytes 16252928 | tf_op jit(solution)/shard_map/dot_general | solution.py:31
  169.2 6.4 %copy.37 = f32[128,5,2048]{2,1,0:T(8,128)} copy(f32[128,5,2048]{2,0,1:T(8,128)S(1)} %fusion.1) | data formatting | bytes 10485760 | tf_op jit(solution)/shard_map/dot_general | solution.py:31
  175.6 7.8 %all-to-all-start.1 = ((f32[128,5,2048]{2,1,0:T(8,128)}), f32[128,5,2048]{2,1,0:T(8,128)}, u32[]{:S(2)}, u32[]{:S(2)}) async-start(f32[128,5,2048]{2,1,0:T(8,128)} %copy.37), calls=%async_computation.1 | async-start | bytes 16777216 | tf_op jit(solution)/shard_map/all_to_all | solution.py:72
  183.5 0.0 all-gather.10.cloned.1.call-start
  183.5 0.5 all-gather.10.cloned.1.call-update
  184.0 0.0 copy-done.7
  184.1 3.3 collective-permute-start.1
  187.4 0.1 iota_compare_fusion
  187.5 0.1 eq.80
  187.6 188.8 %all-to-all-done.1 = f32[128,5,2048]{2,1,0:T(8,128)} async-done(((f32[128,5,2048]{2,1,0:T(8,128)}), f32[128,5,2048]{2,1,0:T(8,128)}, u32[]{:S(2)}, u32[]{:S(2)}) %all-to-all-start.1) | async-done | bytes 5242912 | tf_op jit(solution)/shard_map/all_to_all | solution.py:72
  376.4 6.5 %fusion.5 = f32[64,1,5,2048]{3,2,0,1:T(8,128)} fusion(f32[64,2,5,2048]{3,2,1,0:T(8,128)} %bitcast.5), kind=kLoop, calls=%fused_computation.7 | loop fusion | flops 655360 | bytes 7864320 | tf_op jit(solution)/shard_map/add | solution.py:74
  383.0 4.6 reshape.158
  387.6 3.8 fusion.9
  391.4 0.2 fusion.24
  391.7 0.3 multiply_reduce_fusion
  392.0 0.0 copy-done.3
  392.0 0.3 multiply_convert_fusion
  392.3 0.0 copy-start.2
  392.3 5.7 %collective-permute-start = (bf16[128,2048]{1,0:T(8,128)(2,1)S(1)}, bf16[128,2048]{1,0:T(8,128)(2,1)S(1)}, u32[]{:S(2)}, u32[]{:S(2)}) collective-permute-start(bf16[128,2048]{1,0:T(8,128)(2,1)S(1)} %multiply_convert_fusion), channel_id=1, source_target_pairs={{0,128},{128,0},{1,129},{129,1},{2,130},{130,2},{3,131},{131,3},{4... | collective-permute-start | bytes 1572872 | tf_op jit(solution)/shard_map/ppermute | solution.py:17
  398.0 0.0 collective-permute-done.1
  398.0 0.1 broadcast_compare_fusion
  398.1 0.0 all-gather.12.cloned.1.call-done
  398.1 3.4 fusion.14
  401.6 0.0 all-gather.14.cloned.1.call-done
  401.6 0.0 collective-permute-done
  401.6 2.9 fusion.15
  404.5 0.5 fusion.48
  405.0 0.3 convolution_multiply_fusion.1
  405.4 46.2 %all-gather.10.cloned.1.call-done = bf16[2048,1024]{1,0:T(8,128)(2,1)} async-done(((bf16[8,1024]{1,0:T(8,128)(2,1)}), bf16[2048,1024]{1,0:T(8,128)(2,1)}) %all-gather.10.cloned.1.call-update) | async-done | bytes 4194320 | tf_op jit(solution)/shard_map/all_gather | solution.py:97
  451.6 2.9 convolution_convert_fusion.4
  454.5 0.2 copy.47
  454.7 0.5 convolution_convert_fusion.1
  455.2 1.0 copy.45
  (19 shorter events, 0.1 us)
Async XLA Ops:
  7.2 391.0 %copy-start = (bf16[256,2048]{1,0:T(8,128)(2,1)S(1)}, bf16[256,2048]{1,0:T(8,128)(2,1)}, u32[]{:S(2)}) copy-start(bf16[256,2048]{1,0:T(8,128)(2,1)} %param.19) | copy-start | bytes 3145732
  7.2 2.2 copy-start.4
  7.2 3.5 copy-start.1
  7.2 133.1 %all-gather.6.cloned.1.call-start = ((), (), s32[]{:S(2)}) async-start(), calls=%async_computation.2 | async-start | bytes 12582912 | tf_op jit(solution)/shard_map/all_gather | solution.py:68
  7.9 148.5 %all-gather.8.cloned.1.call-start = ((), (), s32[]{:S(2)}) async-start(), calls=%async_computation.3 | async-start | bytes 12582912 | tf_op jit(solution)/shard_map/all_gather | solution.py:69
  8.7 389.4 %all-gather.12.cloned.1.call-start = ((), (), s32[]{:S(2)}) async-start(), calls=%async_computation.5 | async-start | bytes 4210688 | tf_op jit(solution)/shard_map/all_gather | solution.py:87
  20.9 113.8 %all-to-all-start = ((bf16[128,5,2048]{2,1,0:T(8,128)(2,1)}), bf16[128,5,2048]{2,1,0:T(8,128)(2,1)}, u32[]{:S(2)}, u32[]{:S(2)}) async-start(bf16[128,5,2048]{2,1,0:T(8,128)(2,1)} %bitcast.74), calls=%async_computation | async-start | bytes 8388608 | tf_op jit(solution)/shard_map/all_to_all | solution.py:66
  37.8 363.8 %all-gather.14.cloned.1.call-start = ((), (), s32[]{:S(2)}) async-start(), calls=%async_computation.6 | async-start | bytes 4210688 | tf_op jit(solution)/shard_map/all_gather | solution.py:92
  175.6 8.4 %copy-start.7 = (s32[1,128]{1,0:T(1,128)S(1)}, s32[1,128]{1,0:T(1,128)}, u32[]{:S(2)}) copy-start(s32[1,128]{1,0:T(1,128)} %param.15) | copy-start | bytes 1540
  175.6 200.8 %all-to-all-start.1 = ((f32[128,5,2048]{2,1,0:T(8,128)}), f32[128,5,2048]{2,1,0:T(8,128)}, u32[]{:S(2)}, u32[]{:S(2)}) async-start(f32[128,5,2048]{2,1,0:T(8,128)} %copy.37), calls=%async_computation.1 | async-start | bytes 16777216 | tf_op jit(solution)/shard_map/all_to_all | solution.py:72
  183.5 268.1 %all-gather.10.cloned.1.call-start = ((), (), s32[]{:S(2)}) async-start(), calls=%async_computation.4 | async-start | bytes 4210688 | tf_op jit(solution)/shard_map/all_gather | solution.py:97
  184.1 213.9 %collective-permute-start.1 = (s32[1,128]{1,0:T(1,128)S(1)}, s32[1,128]{1,0:T(1,128)S(1)}, u32[]{:S(2)}, u32[]{:S(2)}) collective-permute-start(s32[1,128]{1,0:T(1,128)S(1)} %copy-done.7), channel_id=1, source_target_pairs={{0,128},{128,0},{1,129},{129,1},{2,130},{130,2},{3,131},{131,3},{4... | collective-permute-start | bytes 1544 | tf_op jit(solution)/shard_map/ppermute | solution.py:17
  383.0 4.6 copy-start.6
  387.6 4.4 copy-start.3
  387.6 10.4 %copy-start.5 = (s32[1,256]{1,0:T(1,128)S(1)}, s32[1,256]{1,0:T(1,128)}, u32[]{:S(2)}) copy-start(s32[1,256]{1,0:T(1,128)} %param.20) | copy-start | bytes 3076
  392.3 9.4 %copy-start.2 = (bf16[128,2048]{1,0:T(8,128)(2,1)}, bf16[128,2048]{1,0:T(8,128)(2,1)S(1)}, u32[]{:S(2)}) copy-start(bf16[128,2048]{1,0:T(8,128)(2,1)S(1)} %multiply_convert_fusion) | copy-start | bytes 1572868
  392.3 9.4 %collective-permute-start = (bf16[128,2048]{1,0:T(8,128)(2,1)S(1)}, bf16[128,2048]{1,0:T(8,128)(2,1)S(1)}, u32[]{:S(2)}, u32[]{:S(2)}) collective-permute-start(bf16[128,2048]{1,0:T(8,128)(2,1)S(1)} %multiply_convert_fusion), channel_id=1, source_target_pairs={{0,128},{128,0},{1,129},{129,1},{2,130},{130,2},{3,131},{131,3},{4... | collective-permute-start | bytes 1572872 | tf_op jit(solution)/shard_map/ppermute | solution.py:17
Sparse Core Ops, SparseCore 0:
  9.8 29.7 all-gather.5
  41.4 26.4 all-gather.7
  71.7 122.8 all-gather.11
  198.2 131.3 all-gather.13
  333.1 118.4 all-gather.9
where the time goes:
time: 463 us
  waiting for transfers between devices  334 us (72%)
  matrix products  39.5 us (9%)
  starting transfers between devices  34.1 us (7%)
  local copies, waits for them, and re-layouts  31.6 us (7%)
  between operations  14 us (3%)
  other arithmetic  9.09 us (2%)
    all_to_all x1, waiting for transfers between devices, body(): lax.all_to_all(half_sum, 'expert', split_axis=0, concat_axis=0, tiled=True)  189 us
    all_to_all x1, waiting for transfers between devices, body(): lax.all_to_all(doubled, 'expert', split_axis=0, concat_axis=0, tiled=True)  96.3 us
    all_gather x1, waiting for transfers between devices, body(): lax.all_gather(value_weight, ('section', 'expert'), axis=0, tiled=True)  46.2 us
    all_to_all x1, starting transfers between devices, body(): lax.all_to_all(doubled, 'expert', split_axis=0, concat_axis=0, tiled=True)  16.9 us
    dot_general x1, matrix products, expert_pass(): return jnp.dot(hidden, second_weight, preferred_element_type=jnp.float32)  12.7 us
    dot_general x2, local copies, waits for them, and re-layouts, expert_pass(): return jnp.dot(hidden, second_weight, preferred_element_type=jnp.float32)  11.9 us
    dot_general x1, matrix products, expert_pass(): jnp.dot(rows, first_weight, preferred_element_type=jnp.float32)  10.7 us
  transfers between devices with their start and end apart: 9, of which 3 were waited for; matrix products, arithmetic and copies ran while one was open for 15% of the time, Pallas kernels for 0%

commit v1 on v0

v1 whole, which is shorter than its diff:
```python
import functools

import jax
import jax.numpy as jnp
from jax import lax
from jax.experimental import pallas as pl
from jax.experimental.pallas import tpu as pltpu
from jax.sharding import PartitionSpec as P

HEADS = 8
HDIM = 128
MESH = pl.DeviceIdType.MESH
CHUNKS = 4
TILE = 256


def layer_norm(values):
    mean = jnp.mean(values, axis=-1, keepdims=True)
    centred = values - mean
    spread = jnp.mean(centred * centred, axis=-1, keepdims=True)
    return centred * lax.rsqrt(spread + 1e-05)


def await_bytes(ref, sem):
    pltpu.make_async_copy(ref, ref, sem).wait()


def expert_kernel(
    packed,
    first,
    second,
    share,
    back,
    gathered,
    rows_in,
    rows,
    w_first,
    w_second,
    hidden,
    result,
    mate_part,
    part_in,
    summed,
    share_in,
    strip,
    d_send,
    d_recv,
    f_send,
    f_recv,
    w_send,
    w_recv,
    w_local,
    p_send,
    p_recv,
    r_send,
    r_recv,
    a_send,
    a_recv,
    c_sem,
):
    s = lax.axis_index("section")
    j = lax.axis_index("expert")
    y, x, z = j // 32, (j // 8) % 4, j % 8
    k = z // 2
    out = 2 * (z % 2) - 1
    mate = z - out
    column = y * 4 + x
    mine = column * 4 + k

    def device(dy, dx, new_z):
        return (s, (((y + dy) % 4) * 4 + (x + dx) % 4) * 8 + new_z)

    def near(q):
        return (z + (0, out, -2 * out, 3 * out)[q] + 8) % 8

    def origin(q):
        return (z + out * q + 8) % 8

    partner = (1 - s, j)
    mate_id = device(0, 0, mate)
    next_id = device(0, 0, origin(1))

    own_first = pltpu.make_async_copy(first.at[0], w_first.at[0], w_local.at[0])
    own_second = pltpu.make_async_copy(second.at[0], w_second.at[0], w_local.at[1])
    own_first.start()
    own_second.start()

    barrier = pltpu.get_barrier_semaphore()
    spread = (0, 1, 2, -2, 3)

    def greet(dy, dx, step):
        pl.semaphore_signal(
            barrier, inc=1, device_id=device(dy, dx, (z + out * step + 8) % 8), device_id_type=MESH
        )

    def greet_column(g, carry):
        for step in spread:
            greet(g // 4, g % 4, step)
        return carry

    lax.fori_loop(1, 16, greet_column, 0)
    for step in spread[1:]:
        greet(0, 0, step)
    pl.semaphore_signal(barrier, inc=1, device_id=mate_id, device_id_type=MESH)
    pl.semaphore_signal(barrier, inc=1, device_id=partner, device_id_type=MESH)
    pl.semaphore_wait(barrier, 81)

    def remote(src, dst, send, recv, to):
        return pltpu.make_async_remote_copy(
            src_ref=src, dst_ref=dst, send_sem=send, recv_sem=recv, device_id=to, device_id_type=MESH
        )

    share_copy = remote(share, share_in, a_send.at[0], a_recv.at[0], mate_id)
    share_copy.start()

    def dispatch(dy, dx, g, q):
        target = near(q)
        expert = (((y + dy) % 4) * 4 + (x + dx) % 4) * 4 + target // 2
        return expert, device(dy, dx, target)

    kept = pltpu.make_async_copy(packed.at[mine], rows_in.at[0, 0, 0], d_recv.at[0])
    kept.start()

    def send_one(dy, dx, g, q):
        expert, to = dispatch(dy, dx, g, q)
        remote(packed.at[expert], rows_in.at[0, g, q], d_send, d_recv.at[g // 4], to).start()

    for q in range(1, 4):
        send_one(0, 0, 0, q)

    def send_column(g, carry):
        for q in range(4):
            send_one(g // 4, g % 4, g, q)
        return carry

    lax.fori_loop(1, 16, send_column, 0)

    w1_copy = remote(first.at[0], w_first.at[1], w_send.at[0], w_recv.at[0], partner)
    w2_copy = remote(second.at[0], w_second.at[1], w_send.at[1], w_recv.at[1], partner)
    w1_copy.start()
    w2_copy.start()

    here = gathered.at[s, y, x]
    plus, minus = (k + out + 4) % 4, (k - out + 4) % 4
    half = strip.shape[1] // 2
    cols = (pl.ds(0, half), pl.ds(half, half))
    xl, xr = (x + 3) % 4, (x + 1) % 4
    yl, yr = (y + 3) % 4, (y + 1) % 4
    ids = {
        "xl": device(0, 3, z),
        "xr": device(0, 1, z),
        "yl": device(3, 0, z),
        "yr": device(1, 0, z),
    }

    def along(ref, n, to):
        return remote(ref, ref, a_send.at[n], a_recv.at[n], to)

    def gather_0():
        share_copy.wait()
        low = jnp.where(z % 2 == 0, share[...], share_in[...])
        high = jnp.where(z % 2 == 0, share_in[...], share[...])
        strip[...] = jnp.concatenate([low, high], axis=0).astype(jnp.bfloat16)
        pltpu.make_async_copy(strip, here.at[k], w_local.at[2]).start()
        remote(strip, here.at[k], a_send.at[1], a_recv.at[1], next_id).start()

    def gather_1():
        await_bytes(here.at[plus], a_recv.at[1])
        along(here.at[plus], 2, mate_id).start()

    def gather_2():
        await_bytes(here.at[minus], a_recv.at[2])
        along(here.at[minus], 3, next_id).start()

    block_a = lambda yy, xx, ks=pl.ds(0, 4): gathered.at[s, yy, xx, ks, :, cols[0]]
    block_b = lambda yy, xx, ks=pl.ds(0, 4): gathered.at[s, yy, xx, ks, :, cols[1]]
    row_a = lambda yy, ks=pl.ds(0, 4): gathered.at[s, yy, :, ks, :, cols[0]]
    row_b = lambda xx, ks=pl.ds(0, 4): gathered.at[s, :, xx, ks, :, cols[1]]
    lo, hi = pl.ds(0, 2), pl.ds(2, 2)

    def gather_3():
        await_bytes(here.at[(k + 2) % 4], a_recv.at[3])
        pltpu.make_async_copy(strip, here.at[k], w_local.at[2]).wait()
        along(block_a(y, x), 4, ids["xr"]).start()
        along(block_a(y, x), 5, ids["xl"]).start()
        along(block_b(y, x), 6, ids["yr"]).start()
        along(block_b(y, x), 7, ids["yl"]).start()

    def gather_4():
        await_bytes(block_a(y, xl), a_recv.at[4])
        along(block_a(y, xl, lo), 8, ids["xr"]).start()
        await_bytes(block_b(yl, x), a_recv.at[6])
        along(block_b(yl, x, lo), 10, ids["yr"]).start()
        await_bytes(block_a(y, xr), a_recv.at[5])
        along(block_a(y, xr, hi), 9, ids["xl"]).start()
        await_bytes(block_b(yr, x), a_recv.at[7])
        along(block_b(yr, x, hi), 11, ids["yl"]).start()

    def gather_5():
        x2, y2 = (x + 2) % 4, (y + 2) % 4
        await_bytes(block_a(y, x2, lo), a_recv.at[8])
        await_bytes(block_a(y, x2, hi), a_recv.at[9])
        along(row_a(y), 12, ids["yr"]).start()
        along(row_a(y), 13, ids["yl"]).start()
        await_bytes(block_b(y2, x, lo), a_recv.at[10])
        await_bytes(block_b(y2, x, hi), a_recv.at[11])
        along(row_b(x), 14, ids["xr"]).start()
        along(row_b(x), 15, ids["xl"]).start()

    def gather_6():
        await_bytes(row_a(yl), a_recv.at[12])
        along(row_a(yl, lo), 16, ids["yr"]).start()
        await_bytes(row_b(xl), a_recv.at[14])
        along(row_b(xl, lo), 18, ids["xr"]).start()
        await_bytes(row_a(yr), a_recv.at[13])
        along(row_a(yr, hi), 17, ids["yl"]).start()
        await_bytes(row_b(xr), a_recv.at[15])
        along(row_b(xr, hi), 19, ids["xl"]).start()

    def gather_7():
        x2, y2 = (x + 2) % 4, (y + 2) % 4
        await_bytes(row_a(y2, lo), a_recv.at[16])
        await_bytes(row_a(y2, hi), a_recv.at[17])
        await_bytes(row_b(x2, lo), a_recv.at[18])
        await_bytes(row_b(x2, hi), a_recv.at[19])
        along(gathered.at[s], 20, partner).start()

    def gather_8():
        await_bytes(gathered.at[1 - s], a_recv.at[20])
        await_bytes(strip, a_send.at[1])
        for n in (2, 3):
            await_bytes(here.at[k], a_send.at[n])
        for n in (4, 5, 6, 7):
            await_bytes(block_a(y, x), a_send.at[n])
        for n in (8, 9, 10, 11):
            await_bytes(block_a(y, x, lo), a_send.at[n])
        for n in (12, 13, 14, 15):
            await_bytes(row_a(y), a_send.at[n])
        for n in (16, 17, 18, 19):
            await_bytes(row_a(y, lo), a_send.at[n])
        await_bytes(gathered.at[s], a_send.at[20])

    groups = 16 // CHUNKS
    count = groups * 4 * 5

    def arrive(c):
        part = pl.ds(c * groups, groups)
        await_bytes(rows_in.at[0, part], d_recv.at[c])
        remote(rows_in.at[0, part], rows_in.at[1, part], f_send, f_recv.at[c], mate_id).start()

    def compute(c):
        part = pl.ds(c * groups, groups)
        await_bytes(rows_in.at[1, part], f_recv.at[c])
        for side in range(2):
            tiles = rows_in[side, part].reshape(count, 16, 128)
            rows[side * count : (side + 1) * count] = tiles.reshape(count, 2048)
        width = w_first.shape[2]

        def up(n, carry):
            for side in range(2):
                at = pl.multiple_of(n * TILE, TILE)
                weight = w_first[side, :, pl.ds(at, TILE)]
                value = jnp.dot(rows[...], weight, preferred_element_type=jnp.float32)
                value = jnp.maximum(value, 0.0).astype(jnp.bfloat16)
                hidden[:, pl.ds(pl.multiple_of(side * width + at, TILE), TILE)] = value
            return carry

        lax.fori_loop(0, width // TILE, up, 0)

        def down(n, carry):
            at = pl.ds(pl.multiple_of(n * TILE, TILE), TILE)
            value = jnp.dot(
                hidden[:, :width], w_second[0, :, at], preferred_element_type=jnp.float32
            ) + jnp.dot(hidden[:, width:], w_second[1, :, at], preferred_element_type=jnp.float32)
            result[:, at] = value.astype(jnp.bfloat16)
            return carry

        lax.fori_loop(0, result.shape[1] // TILE, down, 0)
        shape = (groups, 4, 5, 16, 128)
        mate_part[part] = result[count:].reshape(count, 16, 128).reshape(shape)
        remote(mate_part.at[part], part_in.at[part], p_send, p_recv.at[c], mate_id).start()
        summed[part] = result[:count].reshape(count, 16, 128).reshape(shape)

    def reply(c):
        part = pl.ds(c * groups, groups)
        await_bytes(part_in.at[part], p_recv.at[c])
        total = summed[part].astype(jnp.float32) + part_in[part].astype(jnp.float32)
        summed[part] = total.astype(jnp.bfloat16)

        def send_back(n, carry):
            g = c * groups + n
            for q in range(4):
                to = device(4 - g // 4, 4 - g % 4, origin(q))
                copy = remote(summed.at[g, q], back.at[mine], r_send, r_recv, to)
                if q == 0:

                    @pl.when(g > 0)
                    def _():
                        copy.start()

                    @pl.when(g == 0)
                    def _():
                        pltpu.make_async_copy(summed.at[0, 0], back.at[mine], r_recv).start()

                else:
                    copy.start()
            return carry

        lax.fori_loop(0, groups, send_back, 0)

    steps = (gather_1, gather_2, gather_3, gather_4, gather_5, gather_6)
    gather_0()

    def turn(t, carry):
        for n, step in enumerate(steps):
            pl.when(t == n)(step)
        pl.when(t < CHUNKS)(lambda: arrive(t))

        @pl.when(t == 1)
        def _():
            own_first.wait()
            own_second.wait()
            w1_copy.wait()
            w2_copy.wait()

        pl.when((t >= 1) & (t <= CHUNKS))(lambda: compute(t - 1))
        pl.when(t >= 2)(lambda: reply(t - 2))
        return carry

    lax.fori_loop(0, CHUNKS + 2, turn, 0)
    gather_7()
    await_bytes(back, r_recv)
    await_bytes(back.at[pl.ds(0, 63)], r_send)
    await_bytes(back.at[pl.ds(0, 63)], d_send)
    await_bytes(rows_in.at[0], f_send)
    await_bytes(mate_part, p_send)
    gather_8()


def run_experts(packed, first, second, share):
    bf, f32, dma = jnp.bfloat16, jnp.float32, pltpu.SemaphoreType.DMA
    count = 2 * 320 // CHUNKS
    vmem = pl.BlockSpec(memory_space=pltpu.VMEM)
    hbm = pl.BlockSpec(memory_space=pl.ANY)
    return pl.pallas_call(
        expert_kernel,
        out_shape=(
            jax.ShapeDtypeStruct((64, 5, 16, 128), bf),
            jax.ShapeDtypeStruct((2, 4, 4, 4, 16, 3072), bf),
        ),
        in_specs=[vmem, hbm, hbm, vmem],
        out_specs=(vmem, hbm),
        scratch_shapes=[
            pltpu.VMEM((2, 16, 4, 5, 16, 128), bf),
            pltpu.VMEM((count, 2048), bf),
            pltpu.VMEM((2, 2048, 1024), bf),
            pltpu.VMEM((2, 1024, 2048), bf),
            pltpu.VMEM((count, 2048), bf),
            pltpu.VMEM((count, 2048), bf),
            pltpu.VMEM((16, 4, 5, 16, 128), bf),
            pltpu.VMEM((16, 4, 5, 16, 128), bf),
            pltpu.VMEM((16, 4, 5, 16, 128), bf),
            pltpu.VMEM((8, 3072), f32),
            pltpu.VMEM((16, 3072), bf),
            dma,
            dma((CHUNKS,)),
            dma,
            dma((CHUNKS,)),
            dma((2,)),
            dma((2,)),
            dma((3,)),
            dma,
            dma((CHUNKS,)),
            dma,
            dma,
            dma((21,)),
            dma((21,)),
            dma,
        ],
        compiler_params=pltpu.CompilerParams(
            collective_id=0, has_side_effects=True, vmem_limit_bytes=48 << 20
        ),
        cost_estimate=pl.CostEstimate(
            flops=11 * 10**9, bytes_accessed=40 * 10**6, transcendentals=0
        ),
    )(packed, first, second, share)


def swapped(block, axis):
    return lax.ppermute(block, axis, [(0, 1), (1, 0)])


def body(
    source_tokens,
    routes,
    gates,
    source_sentence,
    expert_in,
    expert_out,
    final_gain,
    target_tokens,
    target_sentence,
    query_weight,
    key_weight,
    value_weight,
):
    experts, capacity = 64, 5
    rows_here, width = source_tokens.shape
    normed = layer_norm(source_tokens.astype(jnp.float32)).astype(jnp.bfloat16)
    flat = routes.reshape(-1)
    picks = (flat[:, None] == jnp.arange(experts, dtype=jnp.int32)[None, :]).astype(jnp.int32)
    places = jnp.sum((jnp.cumsum(picks, axis=0) - 1) * picks, axis=1)
    slot_of = (flat * capacity + places).reshape(rows_here, 2)
    hits = slot_of[:, :, None] == jnp.arange(experts * capacity, dtype=jnp.int32)[None, None, :]
    chosen = (hits[:, 0] | hits[:, 1]).astype(jnp.bfloat16)
    packed = jnp.dot(chosen.T, normed, preferred_element_type=jnp.float32).astype(jnp.bfloat16)
    packed = packed.reshape(experts, capacity, 16, 128)
    share = jnp.concatenate([query_weight, key_weight, value_weight], axis=1).astype(jnp.float32)
    back, gathered = run_experts(packed, expert_in, expert_out, share)
    back = back.reshape(experts * capacity, width)
    weights = gathered.reshape(width, 3072)
    mixing = jnp.sum(jnp.where(hits, gates[:, :, None], 0.0), axis=1)
    high = mixing.astype(jnp.bfloat16)
    low = (mixing - high.astype(jnp.float32)).astype(jnp.bfloat16)
    mixture = jnp.dot(high, back, preferred_element_type=jnp.float32) + jnp.dot(
        low, back, preferred_element_type=jnp.float32
    )
    updated = source_tokens.astype(jnp.float32) + mixture
    memory = (layer_norm(updated) * final_gain).astype(jnp.bfloat16)
    partner_memory, partner_sentence = swapped((memory, source_sentence), "section")
    head_width = query_weight.shape[1]
    target_rows = target_tokens.shape[0]
    key_rows = partner_memory.shape[0]
    queries = jnp.dot(
        target_tokens, weights[:, :head_width], preferred_element_type=jnp.float32
    )
    both = jnp.dot(
        partner_memory, weights[:, head_width:], preferred_element_type=jnp.float32
    ).astype(jnp.bfloat16)
    queries = queries.astype(jnp.bfloat16).reshape(target_rows, HEADS, HDIM)
    keys = both[:, :head_width].reshape(key_rows, HEADS, HDIM)
    values = both[:, head_width:].reshape(key_rows, HEADS, HDIM)
    scores = jnp.einsum("qhd,khd->hqk", queries, keys, preferred_element_type=jnp.float32) * (
        1.0 / HDIM**0.5
    )
    same = (target_sentence[0][:, None] == partner_sentence[0][None, :])[None, :, :]
    scores = jnp.where(same, scores, -jnp.inf)
    peak = jnp.max(scores, axis=-1, keepdims=True)
    raised = jnp.exp(scores - peak)
    probs = (raised / jnp.sum(raised, axis=-1, keepdims=True)).astype(jnp.bfloat16)
    mixed = jnp.einsum("hqk,khd->qhd", probs, values, preferred_element_type=jnp.float32)
    return (memory, mixed.reshape(target_rows, head_width).astype(jnp.bfloat16))


def solution(mesh):
    rows = P(("section", "expert"), None)
    placed = (
        rows,
        rows,
        rows,
        rows,
        P("expert", None, "section"),
        P("expert", "section", None),
        P(),
        rows,
        rows,
        rows,
        rows,
        rows,
    )
    return jax.shard_map(
        body, mesh=mesh, in_specs=placed, out_specs=(rows, rows), check_vma=False
    )
```

time: 463 us -> 159 us (0.34)
  waiting for transfers between devices: 334 us -> 0.01 us
  Pallas kernels: 0 us -> 139 us
  starting transfers between devices: 34.1 us -> 0.6 us
  matrix products: 39.5 us -> 9.44 us
  local copies, waits for them, and re-layouts: 31.6 us -> 3.66 us
  between operations: 14 us -> 0.9 us
    all_to_all x2 -> x0, waiting for transfers between devices: 285 us -> none  [the longest x1 189 us: body(): lax.all_to_all(half_sum, 'expert', split_axis=0, concat_axis=0, tiled=True)]
    pallas_call x0 -> x1, Pallas kernels: none -> 139 us  [run_experts(): pl.pallas_call(expert_kernel, out_shape=(jax.ShapeDtypeStruct((64, 5, 16,...]
    all_gather x5 -> x0, waiting for transfers between devices: 46.3 us -> none  [the longest x1 46.2 us: body(): lax.all_gather(value_weight, ('section', 'expert'), axis=0, tiled=True)]
    dot_general x7 -> x5, matrix products: 38.2 us -> 8.21 us  [the longest x1 4.27 us: body(): jnp.dot(target_tokens, weights[:, :head_width], preferred_element_type=jn...]
    all_to_all x2 -> x0, starting transfers between devices: 24.7 us -> none  [the longest x1 16.9 us: body(): lax.all_to_all(doubled, 'expert', split_axis=0, concat_axis=0, tiled=True)]
    dot_general x2 -> x0, local copies, waits for them, and re-layouts: 11.9 us -> none  [expert_pass(): return jnp.dot(hidden, second_weight, preferred_element_type=jnp.float32)]
    ppermute x2, starting transfers between devices: 9.04 us -> 0.6 us  [swapped(): return lax.ppermute(block, axis, [(0, 1), (1, 0)])]
    add x2 -> x1, other arithmetic: 6.53 us -> 0.71 us  [body(): slot_of = (flat * capacity + places).reshape(rows_here, 2)]
  transfers between devices with their start and end apart: 9 -> 2, of which waited for: 3 -> 0; matrix products, arithmetic and copies ran while one was open for 15% -> 3% of each run, Pallas kernels for 0% -> 0%
where the time goes in v1:
time: 159 us
  Pallas kernels  139 us (87%)
  matrix products  9.44 us (6%)
  other arithmetic  4.69 us (3%)
  local copies, waits for them, and re-layouts  3.66 us (2%)
    pallas_call x1, Pallas kernels, run_experts(): pl.pallas_call(expert_kernel, out_shape=(jax.ShapeDtypeStruct((64, 5, 16,...  139 us
    dot_general x1, matrix products, body(): jnp.dot(target_tokens, weights[:, :head_width], preferred_element_type=jn...  4.27 us
  transfers between devices with their start and end apart: 2, of which 0 were waited for; matrix products, arithmetic and copies ran while one was open for 3% of the time, Pallas kernels for 0%

profile of v1, /device:TPU:1, one launch (start us, length us, event | category | flops | bytes accessed | tf_op | source)
XLA Modules:
  0.0 158.7 jit_solution(10580090214588070442)
XLA Ops:
  0.6 0.0 copy-start
  0.6 0.9 copy.43
  1.5 0.1 eq.61
  1.7 0.1 eq.57
  1.8 0.6 reduce-window.6
  2.4 0.2 slice_reduce_fusion
  2.7 0.1 fusion.41
  2.8 0.1 reduce_sum.66
  2.9 0.1 copy.46
  3.0 0.7 multiply_add_fusion
  3.7 0.1 iota_compare_fusion
  3.7 1.2 convert_reduce_fusion
  4.9 0.0 copy-start.8
  4.9 0.0 copy-start.3
  5.0 0.0 copy-start.4
  5.0 0.0 copy-start.5
  5.0 1.3 fusion.22
  6.3 1.6 %fusion.10 = bf16[40,8,16,128]{3,1,2,0:T(8,128)(2,1)S(1)} fusion(bf16[128,2048]{1,0:T(8,128)(2,1)} %param.12, f32[128]{0:T(128)S(1)} %add_rsqrt_fusion.1, f32[128]{0:T(128)S(1)} %broadcast_multiply_fusion.1, pred[128,2,320]{0,2,1:T(32,128)(4,1)S(1)} %iota_compare_fusion), kind=kOutput, calls=%fused_computation.12 | convolution fusion | flops 169517056 | bytes 1917952 | tf_op jit(solution)/shard_map/dot_general | solution.py:416
  8.0 0.3 copy.57
  8.3 0.0 copy-done.8
  8.3 0.0 copy-done.3
  8.3 0.0 copy-done.4
  8.4 0.0 copy-done.5
  8.4 139.4 %shard_map.131 = (bf16[64,5,16,128]{3,2,1,0:T(8,128)(2,1)S(1)}, bf16[2,4,4,4,16,3072]{5,4,3,2,1,0:T(8,128)(2,1)}) custom-call(bf16[64,5,16,128]{3,2,1,0:T(8,128)(2,1)S(1)} %bitcast.59, bf16[1,2048,1024]{2,1,0:T(8,128)(2,1)} %first.1, bf16[1,1024,2048]{2,1,0:T(8,128)(2,1)} %second.1, f32[8,3072]{1,0:T(8,128)S(1)} %maximum_convert_fusion.share), custom_call_target="tpu_custom_call" | custom-call | flops 11000000512 | bytes 40000000 | tf_op jit(solution)/shard_map/pallas_call | solution.py:345
  147.8 0.0 copy-start.1
  147.8 0.5 fusion.13
  148.2 0.6 copy-done.1
  148.8 0.0 copy-start.6
  148.8 0.0 copy-start.9
  148.8 0.0 copy-start.10
  148.8 0.6 fusion.53
  149.4 0.3 multiply_reduce_fusion
  149.6 0.0 copy-done.6
  149.7 0.2 multiply_convert_fusion
  149.9 0.0 copy-start.2
  149.9 0.2 collective-permute-start
  150.1 0.0 copy-done.9
  150.1 0.4 collective-permute-start.1
  150.5 0.0 copy-done
  150.5 0.0 copy-start.7
  150.5 4.3 %fusion.15 = bf16[1024,256]{1,0:T(8,128)(2,1)S(1)} fusion(bf16[256,2048]{1,0:T(8,128)(2,1)S(1)} %copy-done, bf16[2048,3072]{1,0:T(8,128)(2,1)} %bitcast.66), kind=kOutput, calls=%fused_computation.19 | convolution fusion | flops 1074003968 | bytes 5767168 | tf_op jit(solution)/shard_map/dot_general | solution.py:434
  154.8 0.0 copy-done.2
  154.8 0.0 collective-permute-done.1
  154.8 0.0 copy-done.7
  154.8 0.1 broadcast_compare_fusion
  154.9 0.0 collective-permute-done
  154.9 0.0 copy-done.10
  154.9 1.3 fusion.6
  156.2 0.3 convolution_multiply_fusion
  156.5 0.5 fusion.54
  157.0 0.2 copy.54
  157.2 0.5 convolution_convert_fusion.1
  157.7 1.0 copy.51
  (10 shorter events, 0.2 us)
Async XLA Ops:
  0.6 149.8 %copy-start = (bf16[256,2048]{1,0:T(8,128)(2,1)S(1)}, bf16[256,2048]{1,0:T(8,128)(2,1)}, u32[]{:S(2)}) copy-start(bf16[256,2048]{1,0:T(8,128)(2,1)} %param.19) | copy-start | bytes 3145732
  4.9 3.3 %copy-start.8 = (f32[128,2]{0,1:T(2,128)S(1)}, f32[128,2]{0,1:T(2,128)}, u32[]{:S(2)}) copy-start(f32[128,2]{0,1:T(2,128)} %param.14) | copy-start | bytes 3076
  4.9 3.4 %copy-start.3 = (bf16[8,1024]{1,0:T(8,128)(2,1)S(1)}, bf16[8,1024]{1,0:T(8,128)(2,1)}, u32[]{:S(2)}) copy-start(bf16[8,1024]{1,0:T(8,128)(2,1)} %param.23) | copy-start | bytes 49156
  5.0 3.4 %copy-start.4 = (bf16[8,1024]{1,0:T(8,128)(2,1)S(1)}, bf16[8,1024]{1,0:T(8,128)(2,1)}, u32[]{:S(2)}) copy-start(bf16[8,1024]{1,0:T(8,128)(2,1)} %param.22) | copy-start | bytes 49156
  5.0 3.4 %copy-start.5 = (bf16[8,1024]{1,0:T(8,128)(2,1)S(1)}, bf16[8,1024]{1,0:T(8,128)(2,1)}, u32[]{:S(2)}) copy-start(bf16[8,1024]{1,0:T(8,128)(2,1)} %param.21) | copy-start | bytes 49156
  147.8 1.0 copy-start.1
  148.8 0.8 copy-start.6
  148.8 1.3 copy-start.9
  148.8 6.1 %copy-start.10 = (bf16[2,4,4,4,16,3072]{5,4,3,2,1,0:T(8,128)(2,1)S(1)}, bf16[2,4,4,4,16,3072]{5,4,3,2,1,0:T(8,128)(2,1)}, u32[]{:S(2)}) copy-start(bf16[2,4,4,4,16,3072]{5,4,3,2,1,0:T(8,128)(2,1)} %get-tuple-element.5) | copy-start | bytes 37748740
  149.9 4.9 %copy-start.2 = (bf16[128,2048]{1,0:T(8,128)(2,1)}, bf16[128,2048]{1,0:T(8,128)(2,1)S(1)}, u32[]{:S(2)}) copy-start(bf16[128,2048]{1,0:T(8,128)(2,1)S(1)} %multiply_convert_fusion) | copy-start | bytes 1572868
  149.9 5.0 %collective-permute-start = (bf16[128,2048]{1,0:T(8,128)(2,1)S(1)}, bf16[128,2048]{1,0:T(8,128)(2,1)S(1)}, u32[]{:S(2)}, u32[]{:S(2)}) collective-permute-start(bf16[128,2048]{1,0:T(8,128)(2,1)S(1)} %multiply_convert_fusion), channel_id=1, source_target_pairs={{0,128},{128,0},{1,129},{129,1},{2,130},{130,2},{3,131},{131,3},{4... | collective-permute-start | bytes 1572872 | tf_op jit(solution)/shard_map/ppermute | solution.py:390
  150.1 4.7 %collective-permute-start.1 = (s32[1,128]{1,0:T(1,128)S(1)}, s32[1,128]{1,0:T(1,128)S(1)}, u32[]{:S(2)}, u32[]{:S(2)}) collective-permute-start(s32[1,128]{1,0:T(1,128)S(1)} %copy-done.9), channel_id=1, source_target_pairs={{0,128},{128,0},{1,129},{129,1},{2,130},{130,2},{3,131},{131,3},{4... | collective-permute-start | bytes 1544 | tf_op jit(solution)/shard_map/ppermute | solution.py:390
  150.5 4.3 %copy-start.7 = (s32[1,256]{1,0:T(1,128)S(1)}, s32[1,256]{1,0:T(1,128)}, u32[]{:S(2)}) copy-start(s32[1,256]{1,0:T(1,128)} %param.20) | copy-start | bytes 3076

commit v2 on v1

v2 whole, which is shorter than its diff:
```python
import jax
import jax.numpy as jnp
from jax import lax
from jax.experimental import pallas as pl
from jax.experimental.pallas import tpu as pltpu
from jax.sharding import PartitionSpec as P

HDIM = 128
MESH = pl.DeviceIdType.MESH
CHUNKS = 4
TILE = 256
PLAN = {"norm": ((0, 0),), "route": ((0, 1),), "first": ((0, 2),), "arrived": ((0, 3), (1, 4), (2, 5)), "replied": ((3, 6), (5, 7))}


def layer_norm(values):
    mean = jnp.mean(values, axis=-1, keepdims=True)
    centred = values - mean
    spread = jnp.mean(centred * centred, axis=-1, keepdims=True)
    return centred * lax.rsqrt(spread + 1e-05)


def await_bytes(ref, sem):
    pltpu.make_async_copy(ref, ref, sem).wait()


def layer_kernel(
    source,
    routes,
    gates,
    sentence,
    first,
    second,
    gain,
    target,
    target_sentence,
    wq,
    wk,
    wv,
    memory,
    context,
    normed,
    picked,
    mixing,
    packed,
    rows_in,
    rows,
    w_first,
    w_second,
    hidden,
    result,
    mate_part,
    part_in,
    summed,
    share,
    share_in,
    gathered,
    back,
    straight,
    updated,
    targets,
    queries,
    kv,
    kv_in,
    sentence_in,
    d_send,
    d_recv,
    f_send,
    f_recv,
    w_send,
    w_recv,
    w_local,
    p_send,
    p_recv,
    r_send,
    r_recv,
    a_send,
    a_recv,
    x_send,
    x_recv,
    k_send,
    k_recv,
    s_sem,
):
    f32, bf = jnp.float32, jnp.bfloat16
    s = lax.axis_index("section")
    j = lax.axis_index("expert")
    y, x, z = j // 32, (j // 8) % 4, j % 8
    k = z // 2
    out = 2 * (z % 2) - 1
    mate = z - out
    mine = (y * 4 + x) * 4 + k

    def device(dy, dx, new_z):
        return (s, (((y + dy) % 4) * 4 + (x + dx) % 4) * 8 + new_z)

    def near(q):
        return (z + (0, out, -2 * out, 3 * out)[q] + 8) % 8

    def origin(q):
        return (z + out * q + 8) % 8

    partner = (1 - s, j)
    mate_id = device(0, 0, mate)
    next_id = device(0, 0, origin(1))

    own_first = pltpu.make_async_copy(first.at[0], w_first.at[0], w_local.at[0])
    own_second = pltpu.make_async_copy(second.at[0], w_second.at[0], w_local.at[1])
    own_target = pltpu.make_async_copy(target, targets, w_local.at[2])
    own_first.start()
    own_second.start()
    own_target.start()

    barrier = pltpu.get_barrier_semaphore()
    spread = (0, 1, 2, -2, 3)

    def greet(dy, dx, step):
        pl.semaphore_signal(
            barrier, inc=1, device_id=device(dy, dx, (z + out * step + 8) % 8), device_id_type=MESH
        )

    def greet_column(g, carry):
        for step in spread:
            greet(g // 4, g % 4, step)
        return carry

    lax.fori_loop(1, 16, greet_column, 0)
    for step in spread[1:]:
        greet(0, 0, step)
    pl.semaphore_signal(barrier, inc=1, device_id=mate_id, device_id_type=MESH)
    pl.semaphore_signal(barrier, inc=1, device_id=partner, device_id_type=MESH)
    for n, part in enumerate((wq, wk, wv)):
        share[:, n * 1024 : (n + 1) * 1024] = part[...].astype(f32)
    pl.semaphore_wait(barrier, 81)

    def remote(src, dst, send, recv, to):
        return pltpu.make_async_remote_copy(
            src_ref=src, dst_ref=dst, send_sem=send, recv_sem=recv, device_id=to, device_id_type=MESH
        )

    share_copy = remote(share, share_in, a_send.at[0], a_recv.at[0], mate_id)
    share_copy.start()
    sentence_copy = remote(sentence, sentence_in, s_sem.at[0], s_sem.at[1], partner)
    sentence_copy.start()
    w1_copy = remote(first.at[0], w_first.at[1], w_send.at[0], w_recv.at[0], partner)
    w2_copy = remote(second.at[0], w_second.at[1], w_send.at[1], w_recv.at[1], partner)
    w1_copy.start()
    w2_copy.start()

    here = gathered.at[s, y, x]
    plus, minus = (k + out + 4) % 4, (k - out + 4) % 4
    half = gathered.shape[5] // 2
    cols = (pl.ds(0, half), pl.ds(half, half))
    xl, xr = (x + 3) % 4, (x + 1) % 4
    yl, yr = (y + 3) % 4, (y + 1) % 4
    x2, y2 = (x + 2) % 4, (y + 2) % 4
    id_xl, id_xr = device(0, 3, z), device(0, 1, z)
    id_yl, id_yr = device(3, 0, z), device(1, 0, z)
    every, lo, hi = pl.ds(0, 4), pl.ds(0, 2), pl.ds(2, 2)

    def along(ref, n, to):
        remote(ref, ref, a_send.at[n], a_recv.at[n], to).start()

    def across(ref):
        remote(ref, ref, x_send, x_recv, partner).start()

    def block_a(yy, xx, ks=every):
        return gathered.at[s, yy, xx, ks, :, cols[0]]

    def block_b(yy, xx, ks=every):
        return gathered.at[s, yy, xx, ks, :, cols[1]]

    def row_a(yy, ks=every):
        return gathered.at[s, yy, :, ks, :, cols[0]]

    def row_b(xx, ks=every):
        return gathered.at[s, :, xx, ks, :, cols[1]]

    def gather_0():
        share_copy.wait()
        low = jnp.where(z % 2 == 0, share[...], share_in[...])
        high = jnp.where(z % 2 == 0, share_in[...], share[...])
        gathered[s, y, x, k] = jnp.concatenate([low, high], axis=0).astype(bf)
        along(here.at[k], 1, next_id)

    def gather_1():
        await_bytes(here.at[plus], a_recv.at[1])
        along(here.at[plus], 2, mate_id)

    def gather_2():
        await_bytes(here.at[minus], a_recv.at[2])
        along(here.at[minus], 3, next_id)

    def gather_3():
        await_bytes(here.at[(k + 2) % 4], a_recv.at[3])
        along(block_a(y, x), 4, id_xr)
        along(block_b(y, x), 6, id_yr)
        along(block_a(y, x), 5, id_xl)
        along(block_b(y, x), 7, id_yl)
        across(here)

    def gather_4():
        await_bytes(block_a(y, xl), a_recv.at[4])
        along(block_a(y, xl, lo), 8, id_xr)
        await_bytes(block_b(yl, x), a_recv.at[6])
        along(block_b(yl, x, lo), 10, id_yr)
        await_bytes(block_a(y, xr), a_recv.at[5])
        along(block_a(y, xr, hi), 9, id_xl)
        await_bytes(block_b(yr, x), a_recv.at[7])
        along(block_b(yr, x, hi), 11, id_yl)
        for ref in (block_a(y, xl), block_b(yl, x), block_a(y, xr), block_b(yr, x)):
            across(ref)

    def gather_5():
        await_bytes(block_a(y, x2, lo), a_recv.at[8])
        await_bytes(block_a(y, x2, hi), a_recv.at[9])
        along(row_a(y), 12, id_yr)
        along(row_a(y), 13, id_yl)
        await_bytes(block_b(y2, x, lo), a_recv.at[10])
        await_bytes(block_b(y2, x, hi), a_recv.at[11])
        along(row_b(x), 14, id_xr)
        along(row_b(x), 15, id_xl)
        across(block_a(y, x2))
        across(block_b(y2, x))

    def gather_6():
        await_bytes(row_a(yl), a_recv.at[12])
        along(row_a(yl, lo), 16, id_yr)
        await_bytes(row_b(xl), a_recv.at[14])
        along(row_b(xl, lo), 18, id_xr)
        await_bytes(row_a(yr), a_recv.at[13])
        along(row_a(yr, hi), 17, id_yl)
        await_bytes(row_b(xr), a_recv.at[15])
        along(row_b(xr, hi), 19, id_xl)
        for ref in (row_a(yl), row_b(xl), row_a(yr), row_b(xr)):
            across(ref)

    def gather_7():
        await_bytes(row_a(y2, lo), a_recv.at[16])
        await_bytes(row_a(y2, hi), a_recv.at[17])
        across(row_a(y2))
        await_bytes(row_b(x2, lo), a_recv.at[18])
        await_bytes(row_b(x2, hi), a_recv.at[19])
        across(row_b(x2))

    def gather_done():
        for n in (1, 2, 3):
            await_bytes(here.at[k], a_send.at[n])
        for n in range(4, 8):
            await_bytes(block_a(y, x), a_send.at[n])
        for n in range(8, 12):
            await_bytes(block_a(y, x, lo), a_send.at[n])
        for n in range(12, 16):
            await_bytes(row_a(y), a_send.at[n])
        for n in range(16, 20):
            await_bytes(row_a(y, lo), a_send.at[n])
        await_bytes(gathered.at[s], x_send)

    steps = (gather_0, gather_1, gather_2, gather_3, gather_4, gather_5, gather_6, gather_7)

    def gather(place, t=None):
        for when, step in PLAN.get(place, ()):
            if t is None:
                steps[step]()
            else:
                pl.when(t == when)(steps[step])

    count_t, width = source.shape
    normed[...] = layer_norm(source[...].astype(f32)).astype(bf)
    gather("norm")
    token = lax.broadcasted_iota(jnp.int32, (128, count_t), 1)
    expert = lax.broadcasted_iota(jnp.int32, (128, count_t), 0)
    pick_0 = (routes[0:1, :] == expert).astype(f32)
    pick_1 = (routes[1:2, :] == expert).astype(f32)
    picks = pick_0 + pick_1
    earlier = (expert < token).astype(bf)
    before = jnp.dot(picks.astype(bf), earlier, preferred_element_type=f32)
    slots = packed.shape[0] * packed.shape[1]
    slot = lax.broadcasted_iota(jnp.int32, (picked.shape[0], 128), 0)
    owner = lax.broadcasted_iota(jnp.int32, (picked.shape[0], 128), 1)
    wide = ((slot >= owner * 5) & (slot < owner * 5 + 5)).astype(bf)

    def widen(value):
        return jnp.dot(wide, value.astype(bf), preferred_element_type=f32)

    slot_f = slot.astype(f32)
    place = slot_f - 5.0 * jnp.floor((slot_f + 0.5) * 0.2)
    hits = widen(picks) * (widen(before) == place).astype(f32)
    picked[...] = hits.astype(bf)
    weight = pick_0 * gates[0:1, :] + pick_1 * gates[1:2, :]
    weight_high = weight.astype(bf).astype(f32)
    mixing[0] = (hits * widen(weight_high)).T[:, :slots].astype(bf)
    mixing[1] = (hits * widen(weight - weight_high)).T[:, :slots].astype(bf)
    gather("route")

    kept = pltpu.make_async_copy(packed.at[mine], rows_in.at[0, 0, 0], d_recv.at[0])

    def send_one(dy, dx, q):
        g = dy * 4 + dx
        goal = near(q)
        expert = (((y + dy) % 4) * 4 + (x + dx) % 4) * 4 + goal // 2
        remote(
            packed.at[expert], rows_in.at[0, g, q], d_send, d_recv.at[g], device(dy, dx, goal)
        ).start()

    for dy in range(4):
        block = (y + dy) % 4
        chosen = picked[pl.ds(pl.multiple_of(block * 80, 16), 80), :]
        rows80 = jnp.dot(chosen, normed[...], preferred_element_type=f32).astype(bf)
        packed[pl.ds(block * 16, 16)] = rows80.reshape(80, 16, 128).reshape(16, 5, 16, 128)
        if dy == 0:
            kept.start()
            for q in (2, 3, 1):
                send_one(0, 0, q)

        def send_dx(dx, carry):
            for q in (2, 3, 1, 0):
                send_one(dy, dx, q)
            return carry

        lax.fori_loop(1 if dy == 0 else 0, 4, send_dx, 0)
        if dy == 0:
            gather("first")
    gather("sent")

    groups = 16 // CHUNKS
    count = groups * 4 * 5

    def arrive(c):
        def one(n, carry):
            g = c * groups + n
            await_bytes(rows_in.at[0, g], d_recv.at[g])
            remote(rows_in.at[0, g], rows_in.at[1, g], f_send, f_recv.at[c], mate_id).start()
            return carry

        lax.fori_loop(0, groups, one, 0)

    def compute(c):
        part = pl.ds(c * groups, groups)
        await_bytes(rows_in.at[1, part], f_recv.at[c])
        for side in range(2):
            tiles = rows_in[side, part].reshape(count, 16, 128)
            rows[side * count : (side + 1) * count] = tiles.reshape(count, width)
        depth = w_first.shape[2]

        def up(n, carry):
            for side in range(2):
                at = pl.multiple_of(n * TILE, TILE)
                value = jnp.dot(
                    rows[...], w_first[side, :, pl.ds(at, TILE)], preferred_element_type=f32
                )
                value = jnp.maximum(value, 0.0).astype(bf)
                hidden[:, pl.ds(pl.multiple_of(side * depth + at, TILE), TILE)] = value
            return carry

        lax.fori_loop(0, depth // TILE, up, 0)

        def down(n, carry):
            at = pl.ds(pl.multiple_of(n * TILE, TILE), TILE)
            value = jnp.dot(
                hidden[:, :depth], w_second[0, :, at], preferred_element_type=f32
            ) + jnp.dot(hidden[:, depth:], w_second[1, :, at], preferred_element_type=f32)
            result[:, at] = value.astype(bf)
            return carry

        lax.fori_loop(0, width // TILE, down, 0)
        shape = (groups, 4, 5, 16, 128)
        mate_part[part] = result[count:].reshape(count, 16, 128).reshape(shape)
        remote(mate_part.at[part], part_in.at[part], p_send, p_recv.at[c], mate_id).start()
        summed[part] = result[:count].reshape(count, 16, 128).reshape(shape)

    def reply(c):
        part = pl.ds(c * groups, groups)
        await_bytes(part_in.at[part], p_recv.at[c])
        total = summed[part].astype(f32) + part_in[part].astype(f32)
        summed[part] = total.astype(bf)

        def send_back(n, carry):
            g = c * groups + n
            for q in (2, 3, 1, 0):
                to = device(4 - g // 4, 4 - g % 4, origin(q))
                copy = remote(summed.at[g, q], back.at[mine], r_send, r_recv, to)
                if q == 0:

                    @pl.when(g > 0)
                    def _():
                        copy.start()

                    @pl.when(g == 0)
                    def _():
                        pltpu.make_async_copy(summed.at[0, 0], back.at[mine], r_recv).start()

                else:
                    copy.start()
            return carry

        lax.fori_loop(0, groups, send_back, 0)

    def turn(t, carry):
        gather("turn", t)
        pl.when(t < CHUNKS)(lambda: arrive(t))
        gather("arrived", t)

        @pl.when(t == 1)
        def _():
            own_first.wait()
            own_second.wait()
            w1_copy.wait()
            w2_copy.wait()

        pl.when((t >= 1) & (t <= CHUNKS))(lambda: compute(t - 1))
        gather("computed", t)
        pl.when(t >= 2)(lambda: reply(t - 2))
        gather("replied", t)
        return carry

    lax.fori_loop(0, CHUNKS + 2, turn, 0)
    gather("end")

    own_target.wait()
    sentence_copy.wait()
    await_bytes(gathered.at[1 - s], x_recv)

    def weight_tile(at):
        return gathered[:, :, :, :, :, pl.ds(pl.multiple_of(at, TILE), TILE)].reshape(width, TILE)

    def query(n, carry):
        value = jnp.dot(targets[...], weight_tile(n * TILE), preferred_element_type=f32)
        queries[:, pl.ds(pl.multiple_of(n * TILE, TILE), TILE)] = value.astype(bf)
        return carry

    lax.fori_loop(0, 1024 // TILE, query, 0)
    target_rows = targets.shape[0]
    ids = jnp.broadcast_to(target_sentence[...].astype(f32), (128, target_rows)).T
    same = ids == sentence_in[...].astype(f32)

    await_bytes(back, r_recv)

    def straighten(n, carry):
        tiles = back[pl.ds(n * 16, 16)].reshape(80, 16, 128)
        straight[pl.ds(pl.multiple_of(n * 80, 16), 80), :] = tiles.reshape(80, width)
        return carry

    lax.fori_loop(0, 4, straighten, 0)

    def mix(n, carry):
        at = pl.ds(pl.multiple_of(n * TILE, TILE), TILE)
        part = straight[:, at]
        value = jnp.dot(mixing[0], part, preferred_element_type=f32) + jnp.dot(
            mixing[1], part, preferred_element_type=f32
        )
        updated[:, at] = source[:, at].astype(f32) + value
        return carry

    lax.fori_loop(0, width // TILE, mix, 0)
    memory[...] = (layer_norm(updated[...]) * gain[...]).astype(bf)

    def project(n, carry):
        for side in range(2):
            value = jnp.dot(
                memory[...],
                weight_tile(1024 * (side + 1) + n * TILE),
                preferred_element_type=f32,
            )
            kv[n, side] = value.astype(bf)
        remote(kv.at[n], kv_in.at[n], k_send, k_recv.at[n], partner).start()
        return carry

    lax.fori_loop(0, 4, project, 0)

    def attend(n, carry):
        await_bytes(kv_in.at[n], k_recv.at[n])
        for side in range(TILE // HDIM):
            inner = slice(side * HDIM, (side + 1) * HDIM)
            at = pl.ds(pl.multiple_of(n * TILE + side * HDIM, HDIM), HDIM)
            scores = lax.dot_general(
                queries[:, at],
                kv_in[n, 0, :, inner],
                (((1,), (1,)), ((), ())),
                preferred_element_type=f32,
            ) * (1.0 / HDIM**0.5)
            scores = jnp.where(same, scores, -jnp.inf)
            peak = jnp.max(scores, axis=-1, keepdims=True)
            raised = jnp.exp(scores - peak)
            probs = (raised / jnp.sum(raised, axis=-1, keepdims=True)).astype(bf)
            mixed = jnp.dot(probs, kv_in[n, 1, :, inner], preferred_element_type=f32)
            context[:, at] = mixed.astype(bf)
        return carry

    lax.fori_loop(0, 4, attend, 0)
    await_bytes(kv, k_send)
    await_bytes(back.at[pl.ds(0, 63)], r_send)
    await_bytes(back.at[pl.ds(0, 63)], d_send)
    await_bytes(rows_in.at[0], f_send)
    await_bytes(mate_part, p_send)
    gather_done()


def hand_over(memory, context, memory_out, context_out, sem):
    copies = (
        pltpu.make_async_copy(memory, memory_out, sem.at[0]),
        pltpu.make_async_copy(context, context_out, sem.at[1]),
    )
    for copy in copies:
        copy.start()
    for copy in copies:
        copy.wait()


def body(
    source_tokens,
    routes,
    gates,
    source_sentence,
    expert_in,
    expert_out,
    final_gain,
    target_tokens,
    target_sentence,
    query_weight,
    key_weight,
    value_weight,
):
    bf, f32, dma = jnp.bfloat16, jnp.float32, pltpu.SemaphoreType.DMA
    rows, width = source_tokens.shape
    target_rows = target_tokens.shape[0]
    count = 2 * 320 // CHUNKS
    vmem = pl.BlockSpec(memory_space=pltpu.VMEM)
    hbm = pl.BlockSpec(memory_space=pl.ANY)
    results = pl.pallas_call(
        layer_kernel,
        out_shape=(
            jax.ShapeDtypeStruct((rows, width), bf),
            jax.ShapeDtypeStruct((target_rows, 1024), bf),
        ),
        in_specs=[vmem, vmem, vmem, vmem, hbm, hbm, vmem, hbm, vmem, vmem, vmem, vmem],
        out_specs=(vmem, vmem),
        scratch_shapes=[
            pltpu.VMEM((rows, width), bf),
            pltpu.VMEM((384, rows), bf),
            pltpu.VMEM((2, rows, 320), bf),
            pltpu.VMEM((64, 5, 16, 128), bf),
            pltpu.VMEM((2, 16, 4, 5, 16, 128), bf),
            pltpu.VMEM((count, width), bf),
            pltpu.VMEM((2, width, 1024), bf),
            pltpu.VMEM((2, 1024, width), bf),
            pltpu.VMEM((count, width), bf),
            pltpu.VMEM((count, width), bf),
            pltpu.VMEM((16, 4, 5, 16, 128), bf),
            pltpu.VMEM((16, 4, 5, 16, 128), bf),
            pltpu.VMEM((16, 4, 5, 16, 128), bf),
            pltpu.VMEM((8, 3072), f32),
            pltpu.VMEM((8, 3072), f32),
            pltpu.VMEM((2, 4, 4, 4, 16, 3072), bf),
            pltpu.VMEM((64, 5, 16, 128), bf),
            pltpu.VMEM((320, width), bf),
            pltpu.VMEM((rows, width), f32),
            pltpu.VMEM((target_rows, width), bf),
            pltpu.VMEM((target_rows, 1024), bf),
            pltpu.VMEM((4, 2, rows, TILE), bf),
            pltpu.VMEM((4, 2, rows, TILE), bf),
            pltpu.VMEM((1, rows), jnp.int32),
            dma,
            dma((16,)),
            dma,
            dma((CHUNKS,)),
            dma((2,)),
            dma((2,)),
            dma((3,)),
            dma,
            dma((CHUNKS,)),
            dma,
            dma,
            dma((20,)),
            dma((20,)),
            dma,
            dma,
            dma,
            dma((4,)),
            dma((2,)),
        ],
        compiler_params=pltpu.CompilerParams(
            collective_id=0, has_side_effects=True, vmem_limit_bytes=58 << 20
        ),
        cost_estimate=pl.CostEstimate(
            flops=13 * 10**9, bytes_accessed=20 * 10**6, transcendentals=0
        ),
    )(
        source_tokens,
        routes.T,
        gates.T,
        source_sentence,
        expert_in,
        expert_out,
        final_gain.reshape(1, width),
        target_tokens,
        target_sentence,
        query_weight,
        key_weight,
        value_weight,
    )
    return pl.pallas_call(
        hand_over,
        out_shape=tuple(jax.ShapeDtypeStruct(part.shape, part.dtype) for part in results),
        in_specs=[vmem, vmem],
        out_specs=(hbm, hbm),
        scratch_shapes=[dma((2,))],
    )(*results)


def solution(mesh):
    rows = P(("section", "expert"), None)
    placed = (
        rows,
        rows,
        rows,
        rows,
        P("expert", None, "section"),
        P("expert", "section", None),
        P(),
        rows,
        rows,
        rows,
        rows,
        rows,
    )
    return jax.shard_map(
        body, mesh=mesh, in_specs=placed, out_specs=(rows, rows), check_vma=False
    )
```

time: 159 us -> 126 us (0.79)
  Pallas kernels: 139 us -> 126 us
  matrix products: 9.44 us -> 0 us
  other arithmetic: 4.69 us -> 0 us
  local copies, waits for them, and re-layouts: 3.66 us -> 0 us
    pallas_call x1 -> x2, Pallas kernels: 139 us -> 126 us  [the longest x1 123 us: body(): pl.pallas_call(layer_kernel, out_shape=(jax.ShapeDtypeStruct((rows, width...]
    dot_general x7 -> x0, matrix products: 8.98 us -> none  [the longest x1 4.27 us: body(): jnp.dot(target_tokens, weights[:, :head_width], preferred_element_type=jn...]
    reduce_sum x5 -> x0, other arithmetic: 2.94 us -> none  [the longest x2 1.6 us: layer_norm(): spread = jnp.mean(centred * centred, axis=-1, keepdims=True)]
    unnamed x26 -> x0, local copies, waits for them, and re-layouts: 2.83 us -> none
  transfers between devices with their start and end apart: 2 -> 0, of which waited for: 0 -> 0; matrix products, arithmetic and copies ran while one was open for 3% -> 0% of each run, Pallas kernels for 0% -> 0%
where the time goes in v2:
time: 126 us
  Pallas kernels  126 us (100%)
    pallas_call x1, Pallas kernels, body(): pl.pallas_call(layer_kernel, out_shape=(jax.ShapeDtypeStruct((rows, width...  123 us

profile of v2, /device:TPU:1, one launch (start us, length us, event | category | flops | bytes accessed | tf_op | source)
XLA Modules:
  0.0 126.2 jit_solution(2144124359275952281)
XLA Ops:
  0.6 123.4 %shard_map.131 = (bf16[128,2048]{1,0:T(8,128)(2,1)}, bf16[256,1024]{1,0:T(8,128)(2,1)}) custom-call(bf16[128,2048]{1,0:T(8,128)(2,1)} %source.1, s32[2,128]{1,0:T(2,128)} %bitcast.4, f32[2,128]{1,0:T(2,128)} %bitcast.5, s32[1,128]{1,0:T(1,128)} %sentence.1, bf16[1,2048,1024]{2,1,0:T(8,128)(2,1)} %first.1, bf16[1,1024,2048]{2,1,0:T(8,128)(2,1)} %second.1, ...), custom_call_target="tpu_custom_call" | custom-call | flops 12999999488 | bytes 20000000 | tf_op jit(solution)/shard_map/pallas_call | solution.py:529
  124.0 2.2 %shard_map.132 = (bf16[128,2048]{1,0:T(8,128)(2,1)}, bf16[256,1024]{1,0:T(8,128)(2,1)}) custom-call(bf16[128,2048]{1,0:T(8,128)(2,1)} %get-tuple-element.4.memory, bf16[256,1024]{1,0:T(8,128)(2,1)} %get-tuple-element.5.context), custom_call_target="tpu_custom_call" | custom-call | tf_op jit(solution)/shard_map/pallas_call | solution.py:601

commit v3 on v2

--- a/solution.py
+++ b/solution.py
@@ -9,7 +9,7 @@
 MESH = pl.DeviceIdType.MESH
 CHUNKS = 4
 TILE = 256
-PLAN = {"norm": ((0, 0),), "route": ((0, 1),), "first": ((0, 2),), "arrived": ((0, 3), (1, 4), (2, 5)), "replied": ((3, 6), (5, 7))}
+PLAN = {"norm": ((0, 0),), "route": ((0, 1),), "first": ((0, 2),), "arrived": ((0, 3), (1, 4)), "computed": ((1, 5), (3, 6), (4, 7))}
 
 
 def layer_norm(values):
@@ -36,6 +36,8 @@
     wq,
     wk,
     wv,
+    memory_out,
+    context_out,
     memory,
     context,
     normed,
@@ -80,6 +82,7 @@
     k_send,
     k_recv,
     s_sem,
+    o_sem,
 ):
     f32, bf = jnp.float32, jnp.bfloat16
     s = lax.axis_index("section")
@@ -130,6 +133,33 @@
     pl.semaphore_signal(barrier, inc=1, device_id=partner, device_id_type=MESH)
     for n, part in enumerate((wq, wk, wv)):
         share[:, n * 1024 : (n + 1) * 1024] = part[...].astype(f32)
+    count_t, width = source.shape
+    normed[...] = layer_norm(source[...].astype(f32)).astype(bf)
+    token = lax.broadcasted_iota(jnp.int32, (128, count_t), 1)
+    expert = lax.broadcasted_iota(jnp.int32, (128, count_t), 0)
+    pick_0 = (routes[0:1, :] == expert).astype(f32)
+    pick_1 = (routes[1:2, :] == expert).astype(f32)
+    picks = pick_0 + pick_1
+    earlier = (expert < token).astype(bf)
+    before = jnp.dot(picks.astype(bf), earlier, preferred_element_type=f32)
+    slot = lax.broadcasted_iota(jnp.int32, (picked.shape[0], 128), 0)
+    owner = lax.broadcasted_iota(jnp.int32, (picked.shape[0], 128), 1)
+    wide = ((slot >= owner * 5) & (slot < owner * 5 + 5)).astype(bf)
+
+    def widen(value):
+        return jnp.dot(wide, value.astype(bf), preferred_element_type=f32)
+
+    slot_f = slot.astype(f32)
+    place = slot_f - 5.0 * jnp.floor((slot_f + 0.5) * 0.2)
+    hits = widen(picks) * (widen(before) == place).astype(f32)
+    picked[...] = hits.astype(bf)
+    weight = pick_0 * gates[0:1, :] + pick_1 * gates[1:2, :]
+    weight_high = weight.astype(bf).astype(f32)
+    for n, part in enumerate((weight_high, weight - weight_high)):
+        mixed = (hits * widen(part)).T.astype(bf)
+        for block in range(4):
+            mixing[n, block] = mixed[:, block * 80 : (block + 1) * 80]
+
     pl.semaphore_wait(barrier, 81)
 
     def remote(src, dst, send, recv, to):
@@ -264,32 +294,7 @@
             else:
                 pl.when(t == when)(steps[step])
 
-    count_t, width = source.shape
-    normed[...] = layer_norm(source[...].astype(f32)).astype(bf)
     gather("norm")
-    token = lax.broadcasted_iota(jnp.int32, (128, count_t), 1)
-    expert = lax.broadcasted_iota(jnp.int32, (128, count_t), 0)
-    pick_0 = (routes[0:1, :] == expert).astype(f32)
-    pick_1 = (routes[1:2, :] == expert).astype(f32)
-    picks = pick_0 + pick_1
-    earlier = (expert < token).astype(bf)
-    before = jnp.dot(picks.astype(bf), earlier, preferred_element_type=f32)
-    slots = packed.shape[0] * packed.shape[1]
-    slot = lax.broadcasted_iota(jnp.int32, (picked.shape[0], 128), 0)
-    owner = lax.broadcasted_iota(jnp.int32, (picked.shape[0], 128), 1)
-    wide = ((slot >= owner * 5) & (slot < owner * 5 + 5)).astype(bf)
-
-    def widen(value):
-        return jnp.dot(wide, value.astype(bf), preferred_element_type=f32)
-
-    slot_f = slot.astype(f32)
-    place = slot_f - 5.0 * jnp.floor((slot_f + 0.5) * 0.2)
-    hits = widen(picks) * (widen(before) == place).astype(f32)
-    picked[...] = hits.astype(bf)
-    weight = pick_0 * gates[0:1, :] + pick_1 * gates[1:2, :]
-    weight_high = weight.astype(bf).astype(f32)
-    mixing[0] = (hits * widen(weight_high)).T[:, :slots].astype(bf)
-    mixing[1] = (hits * widen(weight - weight_high)).T[:, :slots].astype(bf)
     gather("route")
 
     kept = pltpu.make_async_copy(packed.at[mine], rows_in.at[0, 0, 0], d_recv.at[0])
@@ -337,9 +342,8 @@
     def compute(c):
         part = pl.ds(c * groups, groups)
         await_bytes(rows_in.at[1, part], f_recv.at[c])
-        for side in range(2):
-            tiles = rows_in[side, part].reshape(count, 16, 128)
-            rows[side * count : (side + 1) * count] = tiles.reshape(count, width)
+        tiles = rows_in[:, part].reshape(2 * count, 16, 128)
+        rows[...] = tiles.reshape(2 * count, width)
         depth = w_first.shape[2]
 
         def up(n, carry):
@@ -364,9 +368,10 @@
 
         lax.fori_loop(0, width // TILE, down, 0)
         shape = (groups, 4, 5, 16, 128)
-        mate_part[part] = result[count:].reshape(count, 16, 128).reshape(shape)
+        tiles = result[...].reshape(2 * count, 16, 128)
+        mate_part[part] = tiles[count:].reshape(shape)
         remote(mate_part.at[part], part_in.at[part], p_send, p_recv.at[c], mate_id).start()
-        summed[part] = result[:count].reshape(count, 16, 128).reshape(shape)
+        summed[part] = tiles[:count].reshape(shape)
 
     def reply(c):
         part = pl.ds(c * groups, groups)
@@ -378,7 +383,7 @@
             g = c * groups + n
             for q in (2, 3, 1, 0):
                 to = device(4 - g // 4, 4 - g % 4, origin(q))
-                copy = remote(summed.at[g, q], back.at[mine], r_send, r_recv, to)
+                copy = remote(summed.at[g, q], back.at[mine], r_send, r_recv.at[g // 4], to)
                 if q == 0:
 
                     @pl.when(g > 0)
@@ -387,7 +392,9 @@
 
                     @pl.when(g == 0)
                     def _():
-                        pltpu.make_async_copy(summed.at[0, 0], back.at[mine], r_recv).start()
+                        pltpu.make_async_copy(
+                            summed.at[0, 0], back.at[mine], r_recv.at[0]
+                        ).start()
 
                 else:
                     copy.start()
@@ -433,26 +440,23 @@
     ids = jnp.broadcast_to(target_sentence[...].astype(f32), (128, target_rows)).T
     same = ids == sentence_in[...].astype(f32)
 
-    await_bytes(back, r_recv)
-
-    def straighten(n, carry):
-        tiles = back[pl.ds(n * 16, 16)].reshape(80, 16, 128)
-        straight[pl.ds(pl.multiple_of(n * 80, 16), 80), :] = tiles.reshape(80, width)
-        return carry
-
-    lax.fori_loop(0, 4, straighten, 0)
-
-    def mix(n, carry):
-        at = pl.ds(pl.multiple_of(n * TILE, TILE), TILE)
-        part = straight[:, at]
-        value = jnp.dot(mixing[0], part, preferred_element_type=f32) + jnp.dot(
-            mixing[1], part, preferred_element_type=f32
-        )
-        updated[:, at] = source[:, at].astype(f32) + value
-        return carry
-
-    lax.fori_loop(0, width // TILE, mix, 0)
+    for dy in range(4):
+        block = (y + dy) % 4
+        part = pl.ds(block * 16, 16)
+        await_bytes(back.at[part], r_recv.at[dy])
+        straight[...] = back[part].reshape(80, 16, 128).reshape(80, width)
+
+        def mix(n, carry):
+            at = pl.ds(pl.multiple_of(n * TILE, TILE), TILE)
+            value = jnp.dot(mixing[0, block], straight[:, at], preferred_element_type=f32)
+            value += jnp.dot(mixing[1, block], straight[:, at], preferred_element_type=f32)
+            before = source[:, at].astype(f32) if dy == 0 else updated[:, at]
+            updated[:, at] = before + value
+            return carry
+
+        lax.fori_loop(0, width // TILE, mix, 0)
     memory[...] = (layer_norm(updated[...]) * gain[...]).astype(bf)
+    pltpu.make_async_copy(memory, memory_out, o_sem.at[4]).start()
 
     def project(n, carry):
         for side in range(2):
@@ -481,13 +485,18 @@
             scores = jnp.where(same, scores, -jnp.inf)
             peak = jnp.max(scores, axis=-1, keepdims=True)
             raised = jnp.exp(scores - peak)
-            probs = (raised / jnp.sum(raised, axis=-1, keepdims=True)).astype(bf)
+            probs = (raised * (1.0 / jnp.sum(raised, axis=-1, keepdims=True))).astype(bf)
             mixed = jnp.dot(probs, kv_in[n, 1, :, inner], preferred_element_type=f32)
             context[:, at] = mixed.astype(bf)
+        done = pl.ds(pl.multiple_of(n * TILE, TILE), TILE)
+        pltpu.make_async_copy(context.at[:, done], context_out.at[:, done], o_sem.at[n]).start()
         return carry
 
     lax.fori_loop(0, 4, attend, 0)
     await_bytes(kv, k_send)
+    for n in range(4):
+        await_bytes(context.at[:, pl.ds(n * TILE, TILE)], o_sem.at[n])
+    await_bytes(memory, o_sem.at[4])
     await_bytes(back.at[pl.ds(0, 63)], r_send)
     await_bytes(back.at[pl.ds(0, 63)], d_send)
     await_bytes(rows_in.at[0], f_send)
@@ -533,11 +542,13 @@
             jax.ShapeDtypeStruct((target_rows, 1024), bf),
         ),
         in_specs=[vmem, vmem, vmem, vmem, hbm, hbm, vmem, hbm, vmem, vmem, vmem, vmem],
-        out_specs=(vmem, vmem),
+        out_specs=(hbm, hbm),
         scratch_shapes=[
             pltpu.VMEM((rows, width), bf),
+            pltpu.VMEM((target_rows, 1024), bf),
+            pltpu.VMEM((rows, width), bf),
             pltpu.VMEM((384, rows), bf),
-            pltpu.VMEM((2, rows, 320), bf),
+            pltpu.VMEM((2, 4, rows, 80), bf),
             pltpu.VMEM((64, 5, 16, 128), bf),
             pltpu.VMEM((2, 16, 4, 5, 16, 128), bf),
             pltpu.VMEM((count, width), bf),
@@ -552,7 +563,7 @@
             pltpu.VMEM((8, 3072), f32),
             pltpu.VMEM((2, 4, 4, 4, 16, 3072), bf),
             pltpu.VMEM((64, 5, 16, 128), bf),
-            pltpu.VMEM((320, width), bf),
+            pltpu.VMEM((80, width), bf),
             pltpu.VMEM((rows, width), f32),
             pltpu.VMEM((target_rows, width), bf),
             pltpu.VMEM((target_rows, 1024), bf),
@@ -569,7 +580,7 @@
             dma,
             dma((CHUNKS,)),
             dma,
-            dma,
+            dma((4,)),
             dma((20,)),
             dma((20,)),
             dma,
@@ -577,6 +588,7 @@
             dma,
             dma((4,)),
             dma((2,)),
+            dma((5,)),
         ],
         compiler_params=pltpu.CompilerParams(
             collective_id=0, has_side_effects=True, vmem_limit_bytes=58 << 20

time: 126 us -> 125 us (level)
  Pallas kernels: 126 us -> 124 us
where the time goes in v3:
time: 125 us
  Pallas kernels  124 us (99%)
    pallas_call x1, Pallas kernels, body(): pl.pallas_call(layer_kernel, out_shape=(jax.ShapeDtypeStruct((rows, width...  122 us

profile of v3, /device:TPU:1, one launch (start us, length us, event | category | flops | bytes accessed | tf_op | source)
XLA Modules:
  0.0 125.1 jit_solution(1950882117232688771)
XLA Ops:
  0.6 122.2 %shard_map.131 = (bf16[128,2048]{1,0:T(8,128)(2,1)}, bf16[256,1024]{1,0:T(8,128)(2,1)}) custom-call(bf16[128,2048]{1,0:T(8,128)(2,1)} %source.1, s32[2,128]{1,0:T(2,128)} %bitcast.4, f32[2,128]{1,0:T(2,128)} %bitcast.5, s32[1,128]{1,0:T(1,128)} %sentence.1, bf16[1,2048,1024]{2,1,0:T(8,128)(2,1)} %first.1, bf16[1,1024,2048]{2,1,0:T(8,128)(2,1)} %second.1, ...), custom_call_target="tpu_custom_call" | custom-call | flops 12999999488 | bytes 20000000 | tf_op jit(solution)/shard_map/pallas_call | solution.py:538
  122.9 2.2 %shard_map.132 = (bf16[128,2048]{1,0:T(8,128)(2,1)}, bf16[256,1024]{1,0:T(8,128)(2,1)}) custom-call(bf16[128,2048]{1,0:T(8,128)(2,1)} %get-tuple-element.4.memory, bf16[256,1024]{1,0:T(8,128)(2,1)} %get-tuple-element.5.context), custom_call_target="tpu_custom_call" | custom-call | tf_op jit(solution)/shard_map/pallas_call | solution.py:613

commit v4 on v3

--- a/solution.py
+++ b/solution.py
@@ -314,11 +314,11 @@
         packed[pl.ds(block * 16, 16)] = rows80.reshape(80, 16, 128).reshape(16, 5, 16, 128)
         if dy == 0:
             kept.start()
-            for q in (2, 3, 1):
+            for q in (3, 2, 1):
                 send_one(0, 0, q)
 
         def send_dx(dx, carry):
-            for q in (2, 3, 1, 0):
+            for q in (3, 2, 1, 0):
                 send_one(dy, dx, q)
             return carry
 
@@ -381,7 +381,7 @@
 
         def send_back(n, carry):
             g = c * groups + n
-            for q in (2, 3, 1, 0):
+            for q in (3, 2, 1, 0):
                 to = device(4 - g // 4, 4 - g % 4, origin(q))
                 copy = remote(summed.at[g, q], back.at[mine], r_send, r_recv.at[g // 4], to)
                 if q == 0:

time: 125 us -> 125 us (level)
  no operation moved by 1% of the time
where the time goes in v4:
time: 125 us
  Pallas kernels  124 us (99%)
    pallas_call x1, Pallas kernels, body(): pl.pallas_call(layer_kernel, out_shape=(jax.ShapeDtypeStruct((rows, width...  122 us

profile of v4, /device:TPU:1, one launch (start us, length us, event | category | flops | bytes accessed | tf_op | source)
XLA Modules:
  0.0 125.0 jit_solution(5207393758071303648)
XLA Ops:
  0.6 122.2 %shard_map.131 = (bf16[128,2048]{1,0:T(8,128)(2,1)}, bf16[256,1024]{1,0:T(8,128)(2,1)}) custom-call(bf16[128,2048]{1,0:T(8,128)(2,1)} %source.1, s32[2,128]{1,0:T(2,128)} %bitcast.4, f32[2,128]{1,0:T(2,128)} %bitcast.5, s32[1,128]{1,0:T(1,128)} %sentence.1, bf16[1,2048,1024]{2,1,0:T(8,128)(2,1)} %first.1, bf16[1,1024,2048]{2,1,0:T(8,128)(2,1)} %second.1, ...), custom_call_target="tpu_custom_call" | custom-call | flops 12999999488 | bytes 20000000 | tf_op jit(solution)/shard_map/pallas_call | solution.py:538
  122.8 2.2 %shard_map.132 = (bf16[128,2048]{1,0:T(8,128)(2,1)}, bf16[256,1024]{1,0:T(8,128)(2,1)}) custom-call(bf16[128,2048]{1,0:T(8,128)(2,1)} %get-tuple-element.4.memory, bf16[256,1024]{1,0:T(8,128)(2,1)} %get-tuple-element.5.context), custom_call_target="tpu_custom_call" | custom-call | tf_op jit(solution)/shard_map/pallas_call | solution.py:613
